TPU v7x, 32 devices: a whole 2x2x4 slice. The times are simulated.
32 devices in a mesh: cfg: 2 (over core), tok: 16 (over z, y, x).
Axes of the slice: x: 2, y: 2, z: 4, core: 2. Of those that a mesh axis runs over, the one named last changes fastest.
Arguments:
- hidden_in: bfloat16 [3072, 1152], P('tok'), may hold values from -6 to 6
- noisy_latent: float32 [3072, 16], P('tok'), may hold values from -6 to 6
- piece_rows: int32 [2, 8], replicated, may hold values from 1 to 192, 1024 in all within a row
- modulation: float32 [2, 2, 8, 1152], P('cfg'), may hold values from -3 to 3
- qkv_weight: bfloat16 [16, 1152, 432], P('tok'), may hold values from -1 to 1, as said below
- proj_weight: bfloat16 [16, 1152, 144], P('tok'), may hold values from -1 to 1, as said below
- up_weight: bfloat16 [16, 1152, 576], P('tok'), may hold values from -1 to 1, as said below
- down_weight: bfloat16 [16, 1152, 576], P('tok'), may hold values from -1 to 1, as said below
- final_weight: bfloat16 [1152, 16], replicated, may hold values from -0.1875 to 0.1875
- guidance: float32 [2], replicated, may hold values from 1.5 to 4.5
- solver_coef: float32 [2, 2], replicated, may hold values from 0.3 to 1.2
Outputs:
- next_latent: float32 [3072, 16], P('tok')
- block_out: bfloat16 [2, 3072, 1152], P('cfg', 'tok')
Inputs may be any that keep to these rules, and one draw needn't show every extreme that they name: Row l of piece_rows sums to 1024; in every row the largest entry is 192. `qkv_weight`: copy i equals copy i % 8. `proj_weight`: copy i equals copy i % 8. `up_weight`: copy i equals copy i % 8. `down_weight`: copy i equals copy i % 8.
All inputs are finite; a program needn't handle non-finite values.
Results may differ from a plain program's by a relative error of at most 0.008.
Values may be sent and summed in bfloat16 or wider, within the bound.
No kernel may reach another device: no remote copies, remote signals or barrier semaphores. Data moves between devices by JAX's collectives and lax.ppermute only.
A program may use at most 64 MiB of HBM per device.

v0:
```python
import jax
import jax.numpy as jnp
from jax import lax
from jax.sharding import PartitionSpec as P

HEAD_DIM = 72
GROUP = 8


def from_partner(block, axis, stride):
    count = lax.axis_size(axis)
    route = []
    for low in range(count):
        high = low | 1 << stride
        if high != low and high < count:
            route += [(low, high), (high, low)]
    return lax.ppermute(block, axis, route)


def layer_norm(values):
    center = values - jnp.mean(values, axis=-1, keepdims=True)
    spread = jnp.mean(center * center, axis=-1, keepdims=True)
    return center / jnp.sqrt(spread + 1e-06)


def modulate(values, shift_vec, scale_vec):
    return layer_norm(values) * (1.0 + scale_vec) + shift_vec


def group_gather(piece):
    member_id = lax.axis_index("tok") % GROUP
    joined = piece
    for bit_pos in range(GROUP.bit_length() - 1):
        partner = from_partner(joined, "tok", bit_pos)
        is_upper = member_id // 2**bit_pos % 2 == 1
        joined = jnp.where(
            is_upper,
            jnp.concatenate([partner, joined], axis=0),
            jnp.concatenate([joined, partner], axis=0),
        )
    return joined


def group_reduce(partial_sums):
    member_id = lax.axis_index("tok") % GROUP
    total = partial_sums
    for bit_pos in reversed(range(GROUP.bit_length() - 1)):
        half_rows = total.shape[0] // 2
        lower = total[:half_rows]
        upper = total[half_rows:]
        is_upper = member_id // 2**bit_pos % 2 == 1
        keep_part = jnp.where(is_upper, upper, lower)
        send_part = jnp.where(is_upper, lower, upper)
        total = keep_part + from_partner(send_part, "tok", bit_pos)
    return total


def attention_terms(attn_in, key_valid, qkv_cols, proj_cols):
    row_count = attn_in.shape[0]
    qkv_now = jnp.dot(attn_in, qkv_cols, preferred_element_type=jnp.float32).astype(jnp.bfloat16)
    local_width = qkv_now.shape[1] // 3
    head_count = local_width // HEAD_DIM
    block_size = 512
    block_count = row_count // block_size
    inv_root = HEAD_DIM ** (-0.5)
    results = []
    for head_pos in range(head_count):
        start = head_pos * HEAD_DIM
        queries = qkv_now[:, start : start + HEAD_DIM].reshape(block_count, block_size, HEAD_DIM)
        keys_head = qkv_now[:, local_width + start : local_width + start + HEAD_DIM]
        values_head = qkv_now[:, 2 * local_width + start : 2 * local_width + start + HEAD_DIM]

        def one_block(query_block):
            scores = (
                lax.dot_general(
                    query_block,
                    keys_head,
                    (((1,), (1,)), ((), ())),
                    preferred_element_type=jnp.float32,
                )
                * inv_root
            )
            scores = jnp.where(key_valid[None, :], scores, -1e30)
            row_peak = jnp.max(scores, axis=-1, keepdims=True)
            exp_scores = jnp.exp(scores - row_peak)
            attn_probs = (exp_scores / jnp.sum(exp_scores, axis=-1, keepdims=True)).astype(
                jnp.bfloat16
            )
            return jnp.dot(attn_probs, values_head, preferred_element_type=jnp.float32).astype(
                jnp.bfloat16
            )

        results.append(lax.map(one_block, queries).reshape(row_count, HEAD_DIM))
    heads_out = jnp.concatenate(results, axis=1)
    return lax.dot_general(
        heads_out, proj_cols, (((1,), (1,)), ((), ())), preferred_element_type=jnp.float32
    )


def mlp_terms(mlp_input, up_cols, down_cols):
    hidden_units = jax.nn.gelu(
        jnp.dot(mlp_input, up_cols, preferred_element_type=jnp.float32), approximate=True
    ).astype(jnp.bfloat16)
    return lax.dot_general(
        hidden_units, down_cols, (((1,), (1,)), ((), ())), preferred_element_type=jnp.float32
    )


def shards(
    hidden_in,
    noisy_latent,
    piece_rows,
    modulation,
    qkv_weight,
    proj_weight,
    up_weight,
    down_weight,
    final_weight,
    guidance,
    solver_coef,
):
    capacity = hidden_in.shape[0]
    device_pos = lax.axis_index("tok")
    cfg_half = lax.axis_index("cfg")
    latent_id = device_pos // GROUP
    member_id = device_pos % GROUP
    counts = lax.dynamic_index_in_dim(piece_rows, latent_id, 0, keepdims=False)
    factors = lax.dynamic_index_in_dim(modulation[0], latent_id, 0, keepdims=False)
    scale_now = lax.dynamic_index_in_dim(guidance, latent_id, 0, keepdims=False)
    coef_pair = lax.dynamic_index_in_dim(solver_coef, latent_id, 0, keepdims=False)
    own_count = lax.dynamic_index_in_dim(counts, member_id, 0, keepdims=False)
    slot_pos = jnp.arange(capacity, dtype=jnp.int32)
    own_valid = slot_pos < own_count
    qkv_cols = qkv_weight[0]
    proj_cols = proj_weight[0]
    up_cols = up_weight[0]
    down_cols = down_weight[0]
    key_valid = (slot_pos[None, :] < counts[:, None]).reshape(-1)
    inputs = hidden_in.astype(jnp.float32)
    attn_in = modulate(inputs, factors[0], factors[1]).astype(jnp.bfloat16)
    attn_part = attention_terms(group_gather(attn_in), key_valid, qkv_cols, proj_cols)
    residual_mid = inputs + factors[2] * group_reduce(attn_part)
    mlp_input = modulate(residual_mid, factors[3], factors[4]).astype(jnp.bfloat16)
    mlp_part = mlp_terms(group_gather(mlp_input), up_cols, down_cols)
    block_rows = (residual_mid + factors[5] * group_reduce(mlp_part)).astype(jnp.bfloat16)
    block_rows = jnp.where(own_valid[:, None], block_rows, jnp.zeros_like(block_rows))
    final_in = modulate(block_rows.astype(jnp.float32), factors[6], factors[7]).astype(jnp.bfloat16)
    noise_pred = jnp.dot(final_in, final_weight, preferred_element_type=jnp.float32)
    weight_now = jnp.where(cfg_half == 0, scale_now, 1.0 - scale_now)
    guided = lax.psum(weight_now * noise_pred, "cfg")
    stepped = coef_pair[0] * noisy_latent - coef_pair[1] * guided
    next_latent = jnp.where(own_valid[:, None], stepped, jnp.zeros_like(stepped))
    return (next_latent, block_rows[None])


def solution(mesh):
    placed = (
        P("tok", None),
        P("tok", None),
        P(),
        P("cfg", None, None, None),
        P("tok", None, None),
        P("tok", None, None),
        P("tok", None, None),
        P("tok", None, None),
        P(),
        P(),
        P(),
    )
    return jax.shard_map(
        shards,
        mesh=mesh,
        in_specs=placed,
        out_specs=(P("tok", None), P("cfg", "tok", None)),
        check_vma=False,
    )
```

profile of v0, /device:TPU:0, one launch (start us, length us, event | category | flops | bytes accessed | tf_op | source)
XLA Modules:
  0.0 438.0 jit_solution(4329998605860592992)
XLA Ops:
  3.2 1.8 fusion.69
  6.3 3.0 collective-permute-start
  9.3 10.2 %collective-permute-done = bf16[192,1152]{1,0:T(8,128)(2,1)S(1)} collective-permute-done((bf16[192,1152]{1,0:T(8,128)(2,1)S(1)}, bf16[192,1152]{1,0:T(8,128)(2,1)S(1)}, u32[]{:S(2)}, u32[]{:S(2)}) %collective-permute-start) | collective-permute-done | bytes 442400 | tf_op jit(solution)/shard_map/ppermute | solution.py:17
  19.8 1.8 collective-permute-start.1
  21.6 19.1 %collective-permute-done.1 = bf16[384,1152]{1,0:T(8,128)(2,1)S(1)} collective-permute-done((bf16[384,1152]{1,0:T(8,128)(2,1)S(1)}, bf16[384,1152]{1,0:T(8,128)(2,1)S(1)}, u32[]{:S(2)}, u32[]{:S(2)}) %collective-permute-start.1) | collective-permute-done | bytes 884768 | tf_op jit(solution)/shard_map/ppermute | solution.py:17
  40.7 1.9 maximum_select_fusion.8
  44.1 37.6 %collective-permute-done.2 = bf16[768,1152]{1,0:T(8,128)(2,1)S(1)} collective-permute-done((bf16[768,1152]{1,0:T(8,128)(2,1)}, bf16[768,1152]{1,0:T(8,128)(2,1)S(1)}, u32[]{:S(2)}, u32[]{:S(2)}) %collective-permute-start.2) | collective-permute-done | bytes 1769504 | tf_op jit(solution)/shard_map/ppermute | solution.py:17
  81.6 4.3 fusion.44
  87.6 7.2 %while.23 = (s32[]{:T(128)}, bf16[3,512,72]{1,2,0:T(8,128)(2,1)S(1)}, bf16[3,512,72]{2,1,0:T(8,128)(2,1)S(1)}, bf16[1536,72]{1,0:T(8,128)(2,1)S(1)}, bf16[1536,72]{1,0:T(8,128)(2,1)}, /*index=5*/s32[8]{0:T(128)S(1)}, s32[]{:T(128)}) while((s32[]{:T(128)}, bf16[3,512,72]{1,2,0:T(8,128)(2,1)S(1)}, ...), condition=%wide.region_9.10_spmd.clone, body=%wide.region_6.9_spmd.clone.sunk | while | flops 232821248 | bytes 11330201 | solution.py:93
  95.3 6.9 %while.22 = (s32[]{:T(128)}, bf16[3,512,72]{1,2,0:T(8,128)(2,1)S(1)}, bf16[3,512,72]{2,1,0:T(8,128)(2,1)S(1)}, bf16[1536,72]{1,0:T(8,128)(2,1)S(1)}, bf16[1536,7...) while((s32[]{:T(128)}, bf16[3,512,72]{1,2,0:T(8,128)(2,1)S(1)}, ...), condition=%wide.region_5.6_spmd.clone, body=%wide.region_2.5_spmd.clone.sunk | while | flops 232821248 | bytes 10445437 | solution.py:93
  105.2 74.7 %collective-permute-done.3 = f32[768,1152]{1,0:T(8,128)S(1)} collective-permute-done((f32[768,1152]{1,0:T(8,128)S(1)}, f32[768,1152]{1,0:T(8,128)S(1)}, u32[]{:S(2)}, u32[]{:S(2)}) %collective-permute-start.3) | collective-permute-done | bytes 3538976 | tf_op jit(solution)/shard_map/ppermute | solution.py:17
  181.4 36.2 %collective-permute-done.4 = f32[384,1152]{1,0:T(8,128)S(1)} collective-permute-done((f32[384,1152]{1,0:T(8,128)S(1)}, f32[384,1152]{1,0:T(8,128)S(1)}, u32[]{:S(2)}, u32[]{:S(2)}) %collective-permute-start.4) | collective-permute-done | bytes 1769504 | tf_op jit(solution)/shard_map/ppermute | solution.py:17
  218.5 17.7 %collective-permute-done.5 = f32[192,1152]{1,0:T(8,128)S(1)} collective-permute-done((f32[192,1152]{1,0:T(8,128)S(1)}, f32[192,1152]{1,0:T(8,128)S(1)}, u32[]{:S(2)}, u32[]{:S(2)}) %collective-permute-start.5) | collective-permute-done | bytes 884768 | tf_op jit(solution)/shard_map/ppermute | solution.py:17
  238.2 8.0 %collective-permute-done.6 = bf16[192,1152]{1,0:T(8,128)(2,1)S(1)} collective-permute-done((bf16[192,1152]{1,0:T(8,128)(2,1)S(1)}, bf16[192,1152]{1,0:T(8,128)(2,1)S(1)}, u32[]{:S(2)}, u32[]{:S(2)}) %collective-permute-start.6) | collective-permute-done | bytes 442400 | tf_op jit(solution)/shard_map/ppermute | solution.py:17
  247.0 14.6 %collective-permute-done.7 = bf16[384,1152]{1,0:T(8,128)(2,1)S(1)} collective-permute-done((bf16[384,1152]{1,0:T(8,128)(2,1)S(1)}, bf16[384,1152]{1,0:T(8,128)(2,1)S(1)}, u32[]{:S(2)}, u32[]{:S(2)}) %collective-permute-start.7) | collective-permute-done | bytes 884768 | tf_op jit(solution)/shard_map/ppermute | solution.py:17
  262.6 33.0 %collective-permute-done.8 = bf16[768,1152]{1,0:T(8,128)(2,1)} collective-permute-done((bf16[768,1152]{1,0:T(8,128)(2,1)S(1)}, bf16[768,1152]{1,0:T(8,128)(2,1)}, u32[]{:S(2)}, u32[]{:S(2)}) %collective-permute-start.8) | collective-permute-done | bytes 1769504 | tf_op jit(solution)/shard_map/ppermute | solution.py:17
  295.6 12.6 %fusion.45 = f32[1536,1152]{1,0:T(8,128)} fusion(bf16[768,1152]{1,0:T(8,128)(2,1)S(1)} %maximum_select_fusion.9, bf16[768,1152]{1,0:T(8,128)(2,1)} %collective-permute-done.8, pred[]{:T(512)S(6)} %eq.42, bf16[1,1152,576]{1,2,0:T(8,128)(2,1)S(1)} %copy-done, bf16[1,1152,576]{1,2,0:T(8,128)(2,1)} %param.21), kind=kOutput, calls=%fused_computation.64 | convolution fusion | flops 4100751360 | bytes 13271041 | tf_op jit(solution)/shard_map/dot_general | solution.py:104
  308.3 3.6 slice_select_fusion
  312.2 69.9 %collective-permute-done.9 = f32[768,1152]{1,0:T(8,128)S(1)} collective-permute-done((f32[768,1152]{1,0:T(8,128)S(1)}, f32[768,1152]{1,0:T(8,128)S(1)}, u32[]{:S(2)}, u32[]{:S(2)}) %collective-permute-start.9) | collective-permute-done | bytes 3538976 | tf_op jit(solution)/shard_map/ppermute | solution.py:17
  382.9 31.3 %collective-permute-done.10 = f32[384,1152]{1,0:T(8,128)S(1)} collective-permute-done((f32[384,1152]{1,0:T(8,128)S(1)}, f32[384,1152]{1,0:T(8,128)S(1)}, u32[]{:S(2)}, u32[]{:S(2)}) %collective-permute-start.10) | collective-permute-done | bytes 1769504 | tf_op jit(solution)/shard_map/ppermute | solution.py:17
  419.6 9.3 %collective-permute-done.11 = f32[192,1152]{1,0:T(8,128)} collective-permute-done((f32[192,1152]{1,0:T(8,128)}, f32[192,1152]{1,0:T(8,128)}, u32[]{:S(2)}, u32[]{:S(2)}) %collective-permute-start.11) | collective-permute-done | bytes 884768 | tf_op jit(solution)/shard_map/ppermute | solution.py:17
  428.9 1.7 convert_reduce_fusion.1
  432.0 3.4 psum.7
  435.4 2.5 subtract_select_fusion
  (114 shorter events, 37.1 us)
Async XLA Ops:
  0.6 295.0 %copy-start = (bf16[1,1152,576]{1,2,0:T(8,128)(2,1)S(1)}, bf16[1,1152,576]{1,2,0:T(8,128)(2,1)}, u32[]{:S(2)}) copy-start(bf16[1,1152,576]{1,2,0:T(8,128)(2,1)} %param.22) | copy-start | bytes 3981316
  5.1 39.0 %copy-start.9 = (s32[2,8]{1,0:T(2,128)S(1)}, s32[2,8]{1,0:T(2,128)}, u32[]{:S(2)}) copy-start(s32[2,8]{1,0:T(2,128)} %param.17) | copy-start | bytes 196
  6.3 13.2 %collective-permute-start = (bf16[192,1152]{1,0:T(8,128)(2,1)S(1)}, bf16[192,1152]{1,0:T(8,128)(2,1)S(1)}, u32[]{:S(2)}, u32[]{:S(2)}) collective-permute-start(bf16[192,1152]{1,0:T(8,128)(2,1)S(1)} %fusion.57), channel_id=1, source_target_pairs={{0,1},{1,0},{2,3},{3,2},{4,5},{5,4},{6,7},{7,6},{8,9},{9,8},{10,11... | collective-permute-start | bytes 1327112 | tf_op jit(solution)/shard_map/ppermute | solution.py:17
  19.8 20.9 %collective-permute-start.1 = (bf16[384,1152]{1,0:T(8,128)(2,1)S(1)}, bf16[384,1152]{1,0:T(8,128)(2,1)S(1)}, u32[]{:S(2)}, u32[]{:S(2)}) collective-permute-start(bf16[384,1152]{1,0:T(8,128)(2,1)S(1)} %maximum_select_fusion.12), channel_id=1, source_target_pairs={{0,2},{2,0},{1,3},{3,1},{4,6},{6,4},{5,7},{7,5},{8,10},{10,8},{9,1... | collective-permute-start | bytes 2654216 | tf_op jit(solution)/shard_map/ppermute | solution.py:17
  42.5 39.1 %collective-permute-start.2 = (bf16[768,1152]{1,0:T(8,128)(2,1)}, bf16[768,1152]{1,0:T(8,128)(2,1)S(1)}, u32[]{:S(2)}, u32[]{:S(2)}) collective-permute-start(bf16[768,1152]{1,0:T(8,128)(2,1)} %maximum_select_fusion.8), channel_id=1, source_target_pairs={{0,4},{4,0},{1,5},{5,1},{2,6},{6,2},{3,7},{7,3},{8,12},{12,8},{9,1... | collective-permute-start | bytes 5308424 | tf_op jit(solution)/shard_map/ppermute | solution.py:17
  90.3 1.3 copy-start.5
  95.3 7.0 %copy-start.6 = (bf16[1,1152,144]{1,2,0:T(8,128)(2,1)S(1)}, bf16[1,1152,144]{1,2,0:T(8,128)(2,1)}, u32[]{:S(2)}) copy-start(bf16[1,1152,144]{1,2,0:T(8,128)(2,1)} %param.20) | copy-start | bytes 995332
  103.9 75.9 %collective-permute-start.3 = (f32[768,1152]{1,0:T(8,128)S(1)}, f32[768,1152]{1,0:T(8,128)S(1)}, u32[]{:S(2)}, u32[]{:S(2)}) collective-permute-start(f32[768,1152]{1,0:T(8,128)S(1)} %slice_select_fusion.1), channel_id=1, source_target_pairs={{0,4},{4,0},{1,5},{5,1},{2,6},{6,2},{3,7},{7,3},{8,12},{12,8},{9,1... | collective-permute-start | bytes 10616840 | tf_op jit(solution)/shard_map/ppermute | solution.py:17
  180.5 55.7 %copy-start.3 = (bf16[192,1152]{1,0:T(8,128)(2,1)S(1)}, bf16[192,1152]{1,0:T(8,128)(2,1)}, u32[]{:S(2)}) copy-start(bf16[192,1152]{1,0:T(8,128)(2,1)} %param.15) | copy-start | bytes 1327108
  180.5 37.1 %collective-permute-start.4 = (f32[384,1152]{1,0:T(8,128)S(1)}, f32[384,1152]{1,0:T(8,128)S(1)}, u32[]{:S(2)}, u32[]{:S(2)}) collective-permute-start(f32[384,1152]{1,0:T(8,128)S(1)} %slice_select_fusion.3), channel_id=1, source_target_pairs={{0,2},{2,0},{1,3},{3,1},{4,6},{6,4},{5,7},{7,5},{8,10},{10,8},{9,1... | collective-permute-start | bytes 5308424 | tf_op jit(solution)/shard_map/ppermute | solution.py:17
  218.0 18.3 %collective-permute-start.5 = (f32[192,1152]{1,0:T(8,128)S(1)}, f32[192,1152]{1,0:T(8,128)S(1)}, u32[]{:S(2)}, u32[]{:S(2)}) collective-permute-start(f32[192,1152]{1,0:T(8,128)S(1)} %slice_select_fusion.5), channel_id=1, source_target_pairs={{0,1},{1,0},{2,3},{3,2},{4,5},{5,4},{6,7},{7,6},{8,9},{9,8},{10,11... | collective-permute-start | bytes 2654216 | tf_op jit(solution)/shard_map/ppermute | solution.py:17
  237.8 8.4 %collective-permute-start.6 = (bf16[192,1152]{1,0:T(8,128)(2,1)S(1)}, bf16[192,1152]{1,0:T(8,128)(2,1)S(1)}, u32[]{:S(2)}, u32[]{:S(2)}) collective-permute-start(bf16[192,1152]{1,0:T(8,128)(2,1)S(1)} %add_convert_fusion.1), channel_id=1, source_target_pairs={{0,1},{1,0},{2,3},{3,2},{4,5},{5,4},{6,7},{7,6},{8,9},{9,8},{10,11... | collective-permute-start | bytes 1327112 | tf_op jit(solution)/shard_map/ppermute | solution.py:17
  246.4 15.2 %collective-permute-start.7 = (bf16[384,1152]{1,0:T(8,128)(2,1)S(1)}, bf16[384,1152]{1,0:T(8,128)(2,1)S(1)}, u32[]{:S(2)}, u32[]{:S(2)}) collective-permute-start(bf16[384,1152]{1,0:T(8,128)(2,1)S(1)} %maximum_select_fusion.13), channel_id=1, source_target_pairs={{0,2},{2,0},{1,3},{3,1},{4,6},{6,4},{5,7},{7,5},{8,10},{10,8},{9,1... | collective-permute-start | bytes 2654216 | tf_op jit(solution)/shard_map/ppermute | solution.py:17
  262.3 33.3 %collective-permute-start.8 = (bf16[768,1152]{1,0:T(8,128)(2,1)S(1)}, bf16[768,1152]{1,0:T(8,128)(2,1)}, u32[]{:S(2)}, u32[]{:S(2)}) collective-permute-start(bf16[768,1152]{1,0:T(8,128)(2,1)S(1)} %maximum_select_fusion.9), channel_id=1, source_target_pairs={{0,4},{4,0},{1,5},{5,1},{2,6},{6,2},{3,7},{7,3},{8,12},{12,8},{9,1... | collective-permute-start | bytes 5308424 | tf_op jit(solution)/shard_map/ppermute | solution.py:17
  308.3 73.8 %copy-start.1 = (f32[1536,1152]{1,0:T(8,128)S(1)}, f32[1536,1152]{1,0:T(8,128)}, u32[]{:S(2)}) copy-start(f32[1536,1152]{1,0:T(8,128)} %fusion.45) | copy-start | bytes 21233668
  311.8 70.2 %collective-permute-start.9 = (f32[768,1152]{1,0:T(8,128)S(1)}, f32[768,1152]{1,0:T(8,128)S(1)}, u32[]{:S(2)}, u32[]{:S(2)}) collective-permute-start(f32[768,1152]{1,0:T(8,128)S(1)} %slice_select_fusion), channel_id=1, source_target_pairs={{0,4},{4,0},{1,5},{5,1},{2,6},{6,2},{3,7},{7,3},{8,12},{12,8},{9,1... | collective-permute-start | bytes 10616840 | tf_op jit(solution)/shard_map/ppermute | solution.py:17
  382.8 33.0 %copy-start.12 = (f32[2]{0:T(128)S(1)}, f32[2]{0:T(128)}, u32[]{:S(2)}) copy-start(f32[2]{0:T(128)} %param.24) | copy-start | bytes 28
  382.8 33.6 %copy-start.10 = (s32[2,8]{1,0:T(2,128)S(1)}, s32[2,8]{1,0:T(2,128)}, u32[]{:S(2)}) copy-start(s32[2,8]{1,0:T(2,128)} %param.17) | copy-start | bytes 196
  382.8 36.1 %copy-start.11 = (f32[2,2]{1,0:T(2,128)S(1)}, f32[2,2]{1,0:T(2,128)}, u32[]{:S(2)}) copy-start(f32[2,2]{1,0:T(2,128)} %param.25) | copy-start | bytes 52
  382.8 31.4 %collective-permute-start.10 = (f32[384,1152]{1,0:T(8,128)S(1)}, f32[384,1152]{1,0:T(8,128)S(1)}, u32[]{:S(2)}, u32[]{:S(2)}) collective-permute-start(f32[384,1152]{1,0:T(8,128)S(1)} %slice_select_fusion.2), channel_id=1, source_target_pairs={{0,2},{2,0},{1,3},{3,1},{4,6},{6,4},{5,7},{7,5},{8,10},{10,8},{9,1... | collective-permute-start | bytes 5308424 | tf_op jit(solution)/shard_map/ppermute | solution.py:17
  415.5 13.4 %collective-permute-start.11 = (f32[192,1152]{1,0:T(8,128)}, f32[192,1152]{1,0:T(8,128)}, u32[]{:S(2)}, u32[]{:S(2)}) collective-permute-start(f32[192,1152]{1,0:T(8,128)} %slice_select_fusion.4), channel_id=1, source_target_pairs={{0,1},{1,0},{2,3},{3,2},{4,5},{5,4},{6,7},{7,6},{8,9},{9,8},{10,11... | collective-permute-start | bytes 2654216 | tf_op jit(solution)/shard_map/ppermute | solution.py:17
  418.9 12.0 %copy-start.8 = (pred[192]{0:T(512)(128)(4,1)}, pred[192]{0:T(512)(128)(4,1)S(1)}, u32[]{:S(2)}) copy-start(pred[192]{0:T(512)(128)(4,1)S(1)} %iota_compare_fusion.2) | copy-start | bytes 580
  430.6 7.4 %copy-start.4 = (bf16[192,1152]{1,0:T(8,128)(2,1)}, bf16[192,1152]{1,0:T(8,128)(2,1)S(1)}, u32[]{:S(2)}) copy-start(bf16[192,1152]{1,0:T(8,128)(2,1)S(1)} %get-tuple-element.155) | copy-start | bytes 1327108
  430.6 4.8 %copy-start.7 = (f32[192,16]{0,1:T(8,128)S(1)}, f32[192,16]{0,1:T(8,128)}, u32[]{:S(2)}) copy-start(f32[192,16]{0,1:T(8,128)} %param.16) | copy-start | bytes 36868
  (3 other events, 3.6 us)
where the time goes:
time: 438 us
  waiting for transfers between devices  362 us (83%)
  matrix products  28.5 us (7%)
  other arithmetic  25.5 us (6%)
  starting transfers between devices  11 us (3%)
  local copies, waits for them, and re-layouts  5.39 us (1%)
    ppermute x12, waiting for transfers between devices, from_partner(): return lax.ppermute(block, axis, route)  362 us
    dot_general x1, matrix products, mlp_terms(): lax.dot_general(hidden_units, down_cols, (((1,), (1,)), ((), ())), prefer...  12.6 us
    ppermute x12, starting transfers between devices, from_partner(): return lax.ppermute(block, axis, route)  11 us
  transfers between devices with their start and end apart: 12, of which 12 were waited for; matrix products, arithmetic and copies ran while one was open for 1% of the time, Pallas kernels for 0%

commit v1 on v0

v1 whole, which is shorter than its diff:
```python
import jax
import jax.numpy as jnp
from jax import lax
from jax.sharding import PartitionSpec as P

HEAD_DIM = 72
GROUP = 8
AXIS_ORDERS = ((1, 2, 4), (2, 4, 1), (4, 1, 2))


def from_member(block, offset):
    count = lax.axis_size("tok")
    return lax.ppermute(block, "tok", [(i, i ^ offset) for i in range(count)])


def from_other_half(block):
    return lax.ppermute(block, "cfg", [(0, 1), (1, 0)])


def after(value, *earlier):
    return lax.optimization_barrier((value,) + earlier)[0]


def layer_norm(values):
    center = values - jnp.mean(values, axis=-1, keepdims=True)
    spread = jnp.mean(center * center, axis=-1, keepdims=True)
    return center / jnp.sqrt(spread + 1e-06)


def modulate(values, shift_vec, scale_vec):
    return layer_norm(values) * (1.0 + scale_vec) + shift_vec


def cube_gather(own_rows):
    piece_rows = own_rows.shape[0] // 3
    first, second, third = [], [], []
    for piece, (b0, b1, b2) in enumerate(AXIS_ORDERS):
        own = own_rows[piece * piece_rows : (piece + 1) * piece_rows]
        first.append((own, b0, b1, b2))
    one = [from_member(own, b0) for own, b0, b1, b2 in first]
    for (own, b0, b1, b2), r1 in zip(first, one):
        second.append(jnp.concatenate([own, r1]))
    two = [from_member(s2, o[2]) for s2, o in zip(second, first)]
    for s2, r2 in zip(second, two):
        third.append(jnp.concatenate([s2, r2]))
    three = [from_member(s3, o[3]) for s3, o in zip(third, first)]
    near = from_other_half(jnp.concatenate([s3[piece_rows:] for s3 in third]))
    far = from_other_half(jnp.concatenate(three))

    def by_offset(s3_of, r3_of):
        found = {}
        for piece, (b0, b1, b2) in enumerate(AXIS_ORDERS):
            order = (0, b0, b1, b0 ^ b1)
            for pos, offset in enumerate(order):
                rows = slice(pos * piece_rows, (pos + 1) * piece_rows)
                if s3_of[piece] is not None:
                    if s3_of[piece].shape[0] == 4 * piece_rows:
                        found[offset, piece] = s3_of[piece][rows]
                    elif pos:
                        found[offset, piece] = s3_of[piece][(pos - 1) * piece_rows : pos * piece_rows]
                found[offset ^ b2, piece] = r3_of[piece][rows]
        return found

    mine = by_offset(third, three)
    other = by_offset(
        [near[3 * i * piece_rows : 3 * (i + 1) * piece_rows] for i in range(3)],
        [far[4 * i * piece_rows : 4 * (i + 1) * piece_rows] for i in range(3)],
    )
    return mine, other, two


def attention(attn_in, key_valid, qkv_cols):
    row_count = attn_in.shape[0]
    qkv_now = jnp.dot(attn_in, qkv_cols, preferred_element_type=jnp.float32).astype(jnp.bfloat16)
    local_width = qkv_now.shape[1] // 3
    head_count = local_width // HEAD_DIM
    block_size = 512
    block_count = row_count // block_size
    inv_root = HEAD_DIM ** (-0.5)
    results = []
    for head_pos in range(head_count):
        start = head_pos * HEAD_DIM
        queries = qkv_now[:, start : start + HEAD_DIM].reshape(block_count, block_size, HEAD_DIM)
        keys_head = qkv_now[:, local_width + start : local_width + start + HEAD_DIM]
        values_head = qkv_now[:, 2 * local_width + start : 2 * local_width + start + HEAD_DIM]

        def one_block(query_block):
            scores = (
                lax.dot_general(
                    query_block,
                    keys_head,
                    (((1,), (1,)), ((), ())),
                    preferred_element_type=jnp.float32,
                )
                * inv_root
            )
            scores = jnp.where(key_valid[None, :], scores, -1e30)
            row_peak = jnp.max(scores, axis=-1, keepdims=True)
            exp_scores = jnp.exp(scores - row_peak)
            attn_probs = (exp_scores / jnp.sum(exp_scores, axis=-1, keepdims=True)).astype(
                jnp.bfloat16
            )
            return jnp.dot(attn_probs, values_head, preferred_element_type=jnp.float32).astype(
                jnp.bfloat16
            )

        results.append(lax.map(one_block, queries).reshape(row_count, HEAD_DIM))
    return jnp.concatenate(results, axis=1)


def shards(
    hidden_in,
    noisy_latent,
    piece_rows,
    modulation,
    qkv_weight,
    proj_weight,
    up_weight,
    down_weight,
    final_weight,
    guidance,
    solver_coef,
):
    capacity = hidden_in.shape[0]
    half_cap = capacity // 2
    device_pos = lax.axis_index("tok")
    cfg_half = lax.axis_index("cfg")
    latent_id = device_pos // GROUP
    member_id = device_pos % GROUP
    counts = lax.dynamic_index_in_dim(piece_rows, latent_id, 0, keepdims=False)
    factors = lax.dynamic_index_in_dim(modulation[0], latent_id, 0, keepdims=False)
    scale_now = lax.dynamic_index_in_dim(guidance, latent_id, 0, keepdims=False)
    coef_pair = lax.dynamic_index_in_dim(solver_coef, latent_id, 0, keepdims=False)
    rel_counts = jnp.stack(
        [lax.dynamic_index_in_dim(counts, member_id ^ d, 0, keepdims=False) for d in range(GROUP)]
    )
    half_pos = jnp.arange(half_cap, dtype=jnp.int32)
    slot_pos = jnp.concatenate([half_pos + cfg_half * half_cap, half_pos + (1 - cfg_half) * half_cap])
    own_valid = slot_pos < rel_counts[0]
    key_valid = (slot_pos[None, :] < rel_counts[:, None]).reshape(-1)

    def swapped(rows):
        mine = lax.dynamic_slice_in_dim(rows, cfg_half * half_cap, half_cap)
        other = lax.dynamic_slice_in_dim(rows, (1 - cfg_half) * half_cap, half_cap)
        return mine, other

    own_mine, own_other = swapped(hidden_in)
    mine, other, stage = cube_gather(own_mine)
    sub = half_cap // 3
    for piece in range(3):
        other[0, piece] = own_other[piece * sub : (piece + 1) * sub]
    gathered = jnp.concatenate(
        [
            part[d, piece]
            for d in range(GROUP)
            for part in (mine, other)
            for piece in range(3)
        ]
    )

    proj_rows = after(proj_weight[0].T, *stage)
    width = proj_rows.shape[0]
    proj_half = lax.dynamic_slice_in_dim(proj_rows, cfg_half * (width // 2), width // 2)
    proj_mine, proj_other, proj_stage = cube_gather(proj_half)
    other_half = lax.dynamic_slice_in_dim(proj_rows, (1 - cfg_half) * (width // 2), width // 2)
    psub = width // 6
    for piece in range(3):
        proj_other[0, piece] = other_half[piece * psub : (piece + 1) * psub]
    first_half = []
    second_half = []
    for d in range(GROUP):
        pm = jnp.concatenate([proj_mine[d, piece] for piece in range(3)])
        po = jnp.concatenate([proj_other[d, piece] for piece in range(3)])
        first_half.append(pm)
        second_half.append(po)
    pm = jnp.stack(first_half)
    po = jnp.stack(second_half)
    lower = jnp.where(cfg_half == 0, pm, po)
    upper = jnp.where(cfg_half == 0, po, pm)
    proj_all = jnp.concatenate([lower, upper], axis=1).reshape(GROUP * width, -1)

    up_cols = up_weight[0]
    down_cols = down_weight[0]
    sent = jnp.where(cfg_half == 0, up_cols, down_cols).T
    sent = after(sent, *stage)
    got = from_member(sent, 4)
    swapped_got = from_other_half(got)
    far_up = jnp.where(cfg_half == 0, got, swapped_got)
    far_down = jnp.where(cfg_half == 0, swapped_got, got)

    attn_in = modulate(gathered.astype(jnp.float32), factors[0], factors[1]).astype(jnp.bfloat16)
    heads_out = attention(attn_in, key_valid, qkv_weight[0])
    heads_t = heads_out.T
    blocks = [heads_t[:, d * capacity : (d + 1) * capacity] for d in range(GROUP)]
    blocks = [blocks[0]] + [from_member(blocks[d], d) for d in range(1, GROUP)]
    heads_flat = jnp.concatenate(blocks)
    attn_out = lax.dot_general(
        heads_flat, proj_all, (((0,), (0,)), ((), ())), preferred_element_type=jnp.float32
    )
    inputs = jnp.concatenate([own_mine, own_other]).astype(jnp.float32)
    residual_mid = inputs + factors[2] * attn_out
    mlp_input = modulate(residual_mid, factors[3], factors[4]).astype(jnp.bfloat16)

    from_x = from_member(mlp_input, 1)
    from_y = from_member(mlp_input, 2)
    diag_low = from_member(from_x[:half_cap], 2)
    diag_high = from_member(from_y[half_cap:], 1)
    rows = jnp.concatenate([mlp_input, from_x, from_y, diag_low, diag_high])
    near_hidden = jax.nn.gelu(
        jnp.dot(rows, up_cols, preferred_element_type=jnp.float32), approximate=True
    ).astype(jnp.bfloat16)
    far_hidden = jax.nn.gelu(
        lax.dot_general(rows, far_up, (((1,), (1,)), ((), ())), preferred_element_type=jnp.float32),
        approximate=True,
    ).astype(jnp.bfloat16)
    partial = lax.dot_general(
        near_hidden, down_cols, (((1,), (1,)), ((), ())), preferred_element_type=jnp.float32
    ) + jnp.dot(far_hidden, far_down, preferred_element_type=jnp.float32)
    own_part = partial[:capacity]
    x_part = partial[capacity : 2 * capacity]
    y_part = partial[2 * capacity : 3 * capacity]
    diag = partial[3 * capacity :].astype(jnp.bfloat16)
    via_x = from_member(diag[:half_cap], 1).astype(jnp.float32)
    via_y = from_member(diag[half_cap:], 2).astype(jnp.float32)
    to_y = jnp.concatenate([y_part[:half_cap] + via_x, y_part[half_cap:]]).astype(jnp.bfloat16)
    to_x = jnp.concatenate([x_part[:half_cap], x_part[half_cap:] + via_y]).astype(jnp.bfloat16)
    mlp_out = (
        own_part
        + from_member(to_x, 1).astype(jnp.float32)
        + from_member(to_y, 2).astype(jnp.float32)
    )
    block_rows = (residual_mid + factors[5] * mlp_out).astype(jnp.bfloat16)
    block_rows = jnp.where(own_valid[:, None], block_rows, jnp.zeros_like(block_rows))
    final_in = modulate(block_rows.astype(jnp.float32), factors[6], factors[7]).astype(jnp.bfloat16)
    noise_pred = jnp.dot(final_in, final_weight, preferred_element_type=jnp.float32)
    noise_pred = jnp.concatenate(swapped(noise_pred))
    block_rows = jnp.concatenate(swapped(block_rows))
    weight_now = jnp.where(cfg_half == 0, scale_now, 1.0 - scale_now)
    weighted = weight_now * noise_pred
    guided = weighted + from_other_half(weighted)
    stepped = coef_pair[0] * noisy_latent - coef_pair[1] * guided
    in_piece = jnp.arange(capacity, dtype=jnp.int32) < rel_counts[0]
    next_latent = jnp.where(in_piece[:, None], stepped, jnp.zeros_like(stepped))
    return (next_latent, block_rows[None])


def solution(mesh):
    placed = (
        P("tok", None),
        P("tok", None),
        P(),
        P("cfg", None, None, None),
        P("tok", None, None),
        P("tok", None, None),
        P("tok", None, None),
        P("tok", None, None),
        P(),
        P(),
        P(),
    )
    return jax.shard_map(
        shards,
        mesh=mesh,
        in_specs=placed,
        out_specs=(P("tok", None), P("cfg", "tok", None)),
        check_vma=False,
    )
```

time: 438 us -> 206 us (0.47)
  waiting for transfers between devices: 362 us -> 83 us
  starting transfers between devices: 11 us -> 40.5 us
  local copies, waits for them, and re-layouts: 5.39 us -> 27.8 us
  other arithmetic: 25.5 us -> 19.2 us
    ppermute x12 -> x40, waiting for transfers between devices: 362 us -> 83 us  [the longest x34 80.9 us: from_member(): return lax.ppermute(block, 'tok', [(i, i ^ offset) for i in range(count)])]
    ppermute x12 -> x40, starting transfers between devices: 11 us -> 40.5 us  [the longest x34 40.4 us: from_member(): return lax.ppermute(block, 'tok', [(i, i ^ offset) for i in range(count)])]
    unnamed x30 -> x94, local copies, waits for them, and re-layouts: 2.85 us -> 13.8 us
    select_n x11 -> x2, other arithmetic: 11 us -> 3.28 us  [the longest x1 1.93 us: shards(): next_latent = jnp.where(in_piece[:, None], stepped, jnp.zeros_like(stepped))]
    another operation x2 -> x3, local copies, waits for them, and re-layouts: 0.04 us -> 5.69 us  [the longest x1 4.96 us: shards(): jnp.stack([lax.dynamic_index_in_dim(counts, member_id ^ d, 0, keepdims=Fa...]
    dot_general x3 -> x4, matrix products: 18.1 us -> 20.2 us  [the longest x1 9.28 us: shards(): jnp.dot(far_hidden, far_down, preferred_element_type=jnp.float32)]
  transfers between devices with their start and end apart: 12 -> 40, of which waited for: 12 -> 23; matrix products, arithmetic and copies ran while one was open for 1% -> 30% of each run, Pallas kernels for 0% -> 0%
where the time goes in v1:
time: 206 us; the launch traced here: 205 us
  waiting for transfers between devices  83 us (40%)
  starting transfers between devices  40.5 us (20%)
  matrix products  31.7 us (15%)
  local copies, waits for them, and re-layouts  27.8 us (13%)
  other arithmetic  19.2 us (9%)
  between operations  2.73 us (1%)
    ppermute x34, waiting for transfers between devices, from_member(): return lax.ppermute(block, 'tok', [(i, i ^ offset) for i in range(count)])  80.9 us
    ppermute x34, starting transfers between devices, from_member(): return lax.ppermute(block, 'tok', [(i, i ^ offset) for i in range(count)])  40.4 us
    unnamed x94, local copies, waits for them, and re-layouts  13.8 us
    dot_general x1, matrix products, shards(): jnp.dot(far_hidden, far_down, preferred_element_type=jnp.float32)  9.28 us
    dot_general x1, matrix products, shards(): lax.dot_general(near_hidden, down_cols, (((1,), (1,)), ((), ())), preferr...  7.19 us
    dot_general x6, matrix products, one_block(): jnp.dot(attn_probs, values_head, preferred_element_type=jnp.float32)  7.02 us
    another operation x1, local copies, waits for them, and re-layouts, shards(): jnp.stack([lax.dynamic_index_in_dim(counts, member_id ^ d, 0, keepdims=Fa...  4.96 us
    dot_general x6, matrix products, one_block(): lax.dot_general(query_block, keys_head, (((1,), (1,)), ((), ())), preferr...  4.19 us
  transfers between devices with their start and end apart: 40, of which 23 were waited for; matrix products, arithmetic and copies ran while one was open for 30% of the time, Pallas kernels for 0%

profile of v1, /device:TPU:0, one launch (start us, length us, event | category | flops | bytes accessed | tf_op | source)
XLA Modules:
  0.0 205.2 jit_solution(9584206840764056768)
XLA Ops:
  1.7 3.0 %collective-permute-start = (bf16[32,1152]{1,0:T(8,128)(2,1)S(1)}, bf16[32,1152]{1,0:T(8,128)(2,1)S(1)}, u32[]{:S(2)}, u32[]{:S(2)}) collective-permute-start(bf16[32,1152]{1,0:T(8,128)(2,1)S(1)} %get-tuple-element.231), channel_id=1, source_target_pairs={{0,1},{1,0},{2,3},{3,2},{4,5},{5,4},{6,7},{7,6},{8,9},{9,8},{10,11... | collective-permute-start | bytes 221192 | tf_op jit(solution)/shard_map/ppermute | solution.py:13
  11.3 3.0 %fusion.52 = bf16[576,1152]{1,0:T(8,128)(2,1)} fusion(bf16[1,1152,576]{1,2,0:T(8,128)(2,1)} %param.22, bf16[1,1152,576]{1,2,0:T(8,128)(2,1)} %param.21, pred[]{:T(512)S(6)} %eq.4), kind=kLoop, calls=%fused_computation.63 | loop fusion | flops 663552 | bytes 3981313 | tf_op jit(solution)/shard_map/transpose | solution.py:184
  15.1 5.0 %stack.65 = s32[8]{0:T(128)S(1)} concatenate(s32[1]{0:T(128)} %bitcast.6, s32[1]{0:T(128)} %bitcast.7, s32[1]{0:T(128)} %bitcast.8, s32[1]{0:T(128)} %bitcast.9, s32[1]{0:T(128)} %bitcast.10, s32[1]{0:T(128)} %bitcast.11, s32[1]{0:T(128)} %bitcast.12, s32[1]{0:T(128)} %bitcast.13), dimensions={0} | concatenate | bytes 64 | tf_op jit(solution)/shard_map/stack | solution.py:134
  22.1 3.3 %collective-permute-done.2 = bf16[64,1152]{1,0:T(8,128)(2,1)S(1)} collective-permute-done((bf16[64,1152]{1,0:T(8,128)(2,1)S(1)}, bf16[64,1152]{1,0:T(8,128)(2,1)S(1)}, u32[]{:S(2)}, u32[]{:S(2)}) %collective-permute-start.2) | collective-permute-done | bytes 147488 | tf_op jit(solution)/shard_map/ppermute | solution.py:13
  27.0 2.5 %collective-permute-start.8 = (bf16[128,1152]{1,0:T(8,128)(2,1)S(1)}, bf16[128,1152]{1,0:T(8,128)(2,1)S(1)}, u32[]{:S(2)}, u32[]{:S(2)}) collective-permute-start(bf16[128,1152]{1,0:T(8,128)(2,1)S(1)} %pad_maximum_fusion.6), channel_id=1, source_target_pairs={{0,4},{1,5},{2,6},{3,7},{4,0},{5,1},{6,2},{7,3},{8,12},{9,13},{10,... | collective-permute-start | bytes 884744 | tf_op jit(solution)/shard_map/ppermute | solution.py:13
  29.7 8.4 %collective-permute-done.22 = bf16[24,1152]{1,0:T(8,128)(2,1)S(1)} collective-permute-done((bf16[24,1152]{1,0:T(8,128)(2,1)S(1)}, bf16[24,1152]{1,0:T(8,128)(2,1)S(1)}, u32[]{:S(2)}, u32[]{:S(2)}) %collective-permute-start.22) | collective-permute-done | bytes 55328 | tf_op jit(solution)/shard_map/ppermute | solution.py:13
  39.6 2.6 %collective-permute-done.19 = bf16[24,1152]{1,0:T(8,128)(2,1)S(1)} collective-permute-done((bf16[24,1152]{1,0:T(8,128)(2,1)S(1)}, bf16[24,1152]{1,0:T(8,128)(2,1)S(1)}, u32[]{:S(2)}, u32[]{:S(2)}) %collective-permute-start.19) | collective-permute-done | bytes 55328 | tf_op jit(solution)/shard_map/ppermute | solution.py:13
  43.4 3.0 %collective-permute-done.18 = bf16[24,1152]{1,0:T(8,128)(2,1)S(1)} collective-permute-done((bf16[24,1152]{1,0:T(8,128)(2,1)S(1)}, bf16[24,1152]{1,0:T(8,128)(2,1)S(1)}, u32[]{:S(2)}, u32[]{:S(2)}) %collective-permute-start.18) | collective-permute-done | bytes 55328 | tf_op jit(solution)/shard_map/ppermute | solution.py:13
  48.2 3.0 %collective-permute-done.20 = bf16[48,1152]{1,0:T(8,128)(2,1)S(1)} collective-permute-done((bf16[48,1152]{1,0:T(8,128)(2,1)S(1)}, bf16[48,1152]{1,0:T(8,128)(2,1)S(1)}, u32[]{:S(2)}, u32[]{:S(2)}) %collective-permute-start.20) | collective-permute-done | bytes 110624 | tf_op jit(solution)/shard_map/ppermute | solution.py:13
  52.4 3.5 %collective-permute-done.23 = bf16[48,1152]{1,0:T(8,128)(2,1)S(1)} collective-permute-done((bf16[48,1152]{1,0:T(8,128)(2,1)S(1)}, bf16[48,1152]{1,0:T(8,128)(2,1)S(1)}, u32[]{:S(2)}, u32[]{:S(2)}) %collective-permute-start.23) | collective-permute-done | bytes 110624 | tf_op jit(solution)/shard_map/ppermute | solution.py:13
  57.5 3.9 %collective-permute-done.24 = bf16[48,1152]{1,0:T(8,128)(2,1)S(1)} collective-permute-done((bf16[48,1152]{1,0:T(8,128)(2,1)S(1)}, bf16[48,1152]{1,0:T(8,128)(2,1)S(1)}, u32[]{:S(2)}, u32[]{:S(2)}) %collective-permute-start.24) | collective-permute-done | bytes 110624 | tf_op jit(solution)/shard_map/ppermute | solution.py:13
  66.7 3.0 %collective-permute-done.21 = bf16[96,1152]{1,0:T(8,128)(2,1)S(1)} collective-permute-done((bf16[96,1152]{1,0:T(8,128)(2,1)S(1)}, bf16[96,1152]{1,0:T(8,128)(2,1)S(1)}, u32[]{:S(2)}, u32[]{:S(2)}) %collective-permute-start.21) | collective-permute-done | bytes 221216 | tf_op jit(solution)/shard_map/ppermute | solution.py:13
  70.8 20.3 %collective-permute-done.26 = bf16[96,1152]{1,0:T(8,128)(2,1)S(1)} collective-permute-done((bf16[96,1152]{1,0:T(8,128)(2,1)S(1)}, bf16[96,1152]{1,0:T(8,128)(2,1)S(1)}, u32[]{:S(2)}, u32[]{:S(2)}) %collective-permute-start.26) | collective-permute-done | bytes 221216 | tf_op jit(solution)/shard_map/ppermute | solution.py:13
  97.3 2.8 %fusion.30 = bf16[1536,432]{0,1:T(8,128)(2,1)S(1)} fusion(bf16[1536,1152]{1,0:T(8,128)(2,1)S(1)} %constant_dynamic-update-slice_fusion.6, f32[1152]{0:T(1024)S(1)} %get-tuple-element.140, f32[1152]{0:T(1024)S(1)} %get-tuple-element.141, f32[1536]{0:T(1024)S(1)} %add_sqrt_fusion, f32[1536]{0:T(1024)S(1)} %broadcast_multiply_fusion, ...), kind=kOutput, calls=%fused_computation.38 | convolution fusion | flops 1540104192 | bytes 5882880 | tf_op jit(solution)/shard_map/dot_general | solution.py:74
  103.5 7.0 %while.23 = (s32[]{:T(128)}, bf16[3,512,72]{1,2,0:T(8,128)(2,1)S(1)}, bf16[3,512,72]{2,1,0:T(8,128)(2,1)S(1)}, bf16[1536,72]{1,0:T(8,128)(2,1)S(1)}, bf16[1536,7...) while((s32[]{:T(128)}, bf16[3,512,72]{1,2,0:T(8,128)(2,1)S(1)}, ...), condition=%wide.region_9.10_spmd.clone, body=%wide.region_6.9_spmd.clone.sunk | while | flops 232821248 | bytes 11330977 | solution.py:107
  115.4 8.8 %while.22 = (s32[]{:T(128)}, bf16[3,512,72]{1,2,0:T(8,128)(2,1)}, bf16[3,512,72]{2,1,0:T(8,128)(2,1)S(1)}, bf16[1536,72]{1,0:T(8,128)(2,1)S(1)}, bf16[1536,72]{1...) while((s32[]{:T(128)}, bf16[3,512,72]{1,2,0:T(8,128)(2,1)}, ...), condition=%wide.region_5.6_spmd.clone, body=%wide.region_2.5_spmd.clone.sunk | while | flops 232821248 | bytes 11158945 | solution.py:107
  131.8 3.3 %collective-permute-start.16 = (bf16[144,192]{1,0:T(8,128)(2,1)S(1)}, bf16[144,192]{1,0:T(8,128)(2,1)S(1)}, u32[]{:S(2)}, u32[]{:S(2)}) collective-permute-start(bf16[144,192]{1,0:T(8,128)(2,1)S(1)} %get-tuple-element.222), channel_id=1, source_target_pairs={{0,6},{1,7},{2,4},{3,5},{4,2},{5,3},{6,0},{7,1},{8,14},{9,15},{10,... | collective-permute-start | bytes 165896 | tf_op jit(solution)/shard_map/ppermute | solution.py:13
  138.6 2.7 %collective-permute-done.17 = bf16[144,192]{1,0:T(8,128)(2,1)S(1)} collective-permute-done((bf16[144,192]{1,0:T(8,128)(2,1)S(1)}, bf16[144,192]{1,0:T(8,128)(2,1)S(1)}, u32[]{:S(2)}, u32[]{:S(2)}) %collective-permute-start.17) | collective-permute-done | bytes 55328 | tf_op jit(solution)/shard_map/ppermute | solution.py:13
  144.5 8.8 %collective-permute-done.29 = bf16[192,1152]{1,0:T(8,128)(2,1)S(1)} collective-permute-done((bf16[192,1152]{1,0:T(8,128)(2,1)S(1)}, bf16[192,1152]{1,0:T(8,128)(2,1)S(1)}, u32[]{:S(2)}, u32[]{:S(2)}) %collective-permute-start.29) | collective-permute-done | bytes 442400 | tf_op jit(solution)/shard_map/ppermute | solution.py:13
  161.9 7.2 %fusion.50 = f32[768,1152]{1,0:T(8,128)} fusion(bf16[1,1152,576]{1,2,0:T(8,128)(2,1)S(1)} %copy-done.3, bf16[768,1152]{1,0:T(8,128)(2,1)} %constant_dynamic-update-slice_fusion.80, bf16[1,1152,576]{1,2,0:T(8,128)(2,1)} %param.21), kind=kOutput, calls=%fused_computation.61 | convolution fusion | flops 2042413056 | bytes 7962624 | tf_op jit(solution)/shard_map/dot_general | solution.py:216
  169.1 9.3 %fusion.124 = (bf16[768,1152]{1,0:T(8,128)(2,1)}, f32[768,1152]{1,0:T(8,128)}) fusion(f32[768,1152]{1,0:T(8,128)} %fusion.50, bf16[576,1152]{1,0:T(8,128)(2,1)} %collective-permute-done.34, bf16[576,1152]{1,0:T(8,128)(2,1)} %collective-permute-done.33, pred[]{:T(512)S(6)} %eq.4, bf16[768,1152]{1,0:T(8,128)(2,1)} %constant_dynamic-update-slice_fusion.80), kind=kOutput, calls=%fused_computation.285 | convolution fusion | flops 2045509632 | bytes 13271041 | tf_op jit(solution)/shard_map/dot_general | solution.py:218
  183.0 4.6 %collective-permute-done.35 = bf16[96,1152]{1,0:T(8,128)(2,1)S(1)} collective-permute-done((bf16[96,1152]{1,0:T(8,128)(2,1)S(1)}, bf16[96,1152]{1,0:T(8,128)(2,1)S(1)}, u32[]{:S(2)}, u32[]{:S(2)}) %collective-permute-start.35) | collective-permute-done | bytes 221216 | tf_op jit(solution)/shard_map/ppermute | solution.py:13
  188.9 2.3 %collective-permute-start.38 = (bf16[192,1152]{1,0:T(8,128)(2,1)S(1)}, bf16[192,1152]{1,0:T(8,128)(2,1)S(1)}, u32[]{:S(2)}, u32[]{:S(2)}) collective-permute-start(bf16[192,1152]{1,0:T(8,128)(2,1)S(1)} %pad_maximum_fusion.4), channel_id=1, source_target_pairs={{0,2},{1,3},{2,0},{3,1},{4,6},{5,7},{6,4},{7,5},{8,10},{9,11},{10,... | collective-permute-start | bytes 1327112 | tf_op jit(solution)/shard_map/ppermute | solution.py:13
  194.2 3.3 %collective-permute-done.38 = bf16[192,1152]{1,0:T(8,128)(2,1)S(1)} collective-permute-done((bf16[192,1152]{1,0:T(8,128)(2,1)S(1)}, bf16[192,1152]{1,0:T(8,128)(2,1)S(1)}, u32[]{:S(2)}, u32[]{:S(2)}) %collective-permute-start.38) | collective-permute-done | bytes 442400 | tf_op jit(solution)/shard_map/ppermute | solution.py:13
  (284 shorter events, 93.7 us)
Async XLA Ops:
  1.7 19.6 %collective-permute-start = (bf16[32,1152]{1,0:T(8,128)(2,1)S(1)}, bf16[32,1152]{1,0:T(8,128)(2,1)S(1)}, u32[]{:S(2)}, u32[]{:S(2)}) collective-permute-start(bf16[32,1152]{1,0:T(8,128)(2,1)S(1)} %get-tuple-element.231), channel_id=1, source_target_pairs={{0,1},{1,0},{2,3},{3,2},{4,5},{5,4},{6,7},{7,6},{8,9},{9,8},{10,11... | collective-permute-start | bytes 221192 | tf_op jit(solution)/shard_map/ppermute | solution.py:13
  4.7 15.4 %collective-permute-start.1 = (bf16[32,1152]{1,0:T(8,128)(2,1)S(1)}, bf16[32,1152]{1,0:T(8,128)(2,1)S(1)}, u32[]{:S(2)}, u32[]{:S(2)}) collective-permute-start(bf16[32,1152]{1,0:T(8,128)(2,1)S(1)} %get-tuple-element.230), channel_id=1, source_target_pairs={{0,2},{1,3},{2,0},{3,1},{4,6},{5,7},{6,4},{7,5},{8,10},{9,11},{10,... | collective-permute-start | bytes 221192 | tf_op jit(solution)/shard_map/ppermute | solution.py:13
  6.3 14.4 %collective-permute-start.4 = (bf16[32,1152]{1,0:T(8,128)(2,1)S(1)}, bf16[32,1152]{1,0:T(8,128)(2,1)S(1)}, u32[]{:S(2)}, u32[]{:S(2)}) collective-permute-start(bf16[32,1152]{1,0:T(8,128)(2,1)S(1)} %get-tuple-element.229), channel_id=1, source_target_pairs={{0,4},{1,5},{2,6},{3,7},{4,0},{5,1},{6,2},{7,3},{8,12},{9,13},{10,... | collective-permute-start | bytes 221192 | tf_op jit(solution)/shard_map/ppermute | solution.py:13
  25.4 38.2 %collective-permute-start.3 = (bf16[128,1152]{1,0:T(8,128)(2,1)S(1)}, bf16[128,1152]{1,0:T(8,128)(2,1)S(1)}, u32[]{:S(2)}, u32[]{:S(2)}) collective-permute-start(bf16[128,1152]{1,0:T(8,128)(2,1)S(1)} %pad_maximum_fusion.5), channel_id=1, source_target_pairs={{0,1},{1,0},{2,3},{3,2},{4,5},{5,4},{6,7},{7,6},{8,9},{9,8},{10,11... | collective-permute-start | bytes 884744 | tf_op jit(solution)/shard_map/ppermute | solution.py:13
  26.7 64.8 %collective-permute-start.7 = (bf16[288,1152]{1,0:T(8,128)(2,1)S(1)}, bf16[288,1152]{1,0:T(8,128)(2,1)S(1)}, u32[]{:S(2)}, u32[]{:S(2)}) collective-permute-start(bf16[288,1152]{1,0:T(8,128)(2,1)S(1)} %constant_dynamic-update-slice_fusion), channel_id=1, source_target_pairs={{0,16},{16,0},{1,17},{17,1},{2,18},{18,2},{3,19},{19,3},{4,20},{20... | collective-permute-start | bytes 1990664 | tf_op jit(solution)/shard_map/ppermute | solution.py:17
  26.8 38.0 %collective-permute-start.9 = (bf16[128,1152]{1,0:T(8,128)(2,1)S(1)}, bf16[128,1152]{1,0:T(8,128)(2,1)S(1)}, u32[]{:S(2)}, u32[]{:S(2)}) collective-permute-start(bf16[128,1152]{1,0:T(8,128)(2,1)S(1)} %pad_maximum_fusion.7), channel_id=1, source_target_pairs={{0,2},{1,3},{2,0},{3,1},{4,6},{5,7},{6,4},{7,5},{8,10},{9,11},{10,... | collective-permute-start | bytes 884744 | tf_op jit(solution)/shard_map/ppermute | solution.py:13
  27.0 39.4 %collective-permute-start.8 = (bf16[128,1152]{1,0:T(8,128)(2,1)S(1)}, bf16[128,1152]{1,0:T(8,128)(2,1)S(1)}, u32[]{:S(2)}, u32[]{:S(2)}) collective-permute-start(bf16[128,1152]{1,0:T(8,128)(2,1)S(1)} %pad_maximum_fusion.6), channel_id=1, source_target_pairs={{0,4},{1,5},{2,6},{3,7},{4,0},{5,1},{6,2},{7,3},{8,12},{9,13},{10,... | collective-permute-start | bytes 884744 | tf_op jit(solution)/shard_map/ppermute | solution.py:13
  29.5 8.5 %collective-permute-start.22 = (bf16[24,1152]{1,0:T(8,128)(2,1)S(1)}, bf16[24,1152]{1,0:T(8,128)(2,1)S(1)}, u32[]{:S(2)}, u32[]{:S(2)}) collective-permute-start(bf16[24,1152]{1,0:T(8,128)(2,1)S(1)} %get-tuple-element.234), channel_id=1, source_target_pairs={{0,4},{1,5},{2,6},{3,7},{4,0},{5,1},{6,2},{7,3},{8,12},{9,13},{10,... | collective-permute-start | bytes 165896 | tf_op jit(solution)/shard_map/ppermute | solution.py:13
  61.4 83.1 %collective-permute-start.33 = (bf16[576,1152]{1,0:T(8,128)(2,1)}, bf16[576,1152]{1,0:T(8,128)(2,1)}, u32[]{:S(2)}, u32[]{:S(2)}) collective-permute-start(bf16[576,1152]{1,0:T(8,128)(2,1)} %fusion.52), channel_id=1, source_target_pairs={{0,4},{1,5},{2,6},{3,7},{4,0},{5,1},{6,2},{7,3},{8,12},{9,13},{10,... | collective-permute-start | bytes 3981320 | tf_op jit(solution)/shard_map/ppermute | solution.py:13
  63.7 6.0 %collective-permute-start.21 = (bf16[96,1152]{1,0:T(8,128)(2,1)S(1)}, bf16[96,1152]{1,0:T(8,128)(2,1)S(1)}, u32[]{:S(2)}, u32[]{:S(2)}) collective-permute-start(bf16[96,1152]{1,0:T(8,128)(2,1)S(1)} %pad_maximum_fusion.8), channel_id=1, source_target_pairs={{0,1},{1,0},{2,3},{3,2},{4,5},{5,4},{6,7},{7,6},{8,9},{9,8},{10,11... | collective-permute-start | bytes 663560 | tf_op jit(solution)/shard_map/ppermute | solution.py:13
  66.4 24.8 %collective-permute-start.26 = (bf16[96,1152]{1,0:T(8,128)(2,1)S(1)}, bf16[96,1152]{1,0:T(8,128)(2,1)S(1)}, u32[]{:S(2)}, u32[]{:S(2)}) collective-permute-start(bf16[96,1152]{1,0:T(8,128)(2,1)S(1)} %pad_maximum_fusion.10), channel_id=1, source_target_pairs={{0,4},{1,5},{2,6},{3,7},{4,0},{5,1},{6,2},{7,3},{8,12},{9,13},{10,... | collective-permute-start | bytes 663560 | tf_op jit(solution)/shard_map/ppermute | solution.py:13
  69.7 21.9 %collective-permute-start.27 = (bf16[216,1152]{1,0:T(8,128)(2,1)S(1)}, bf16[216,1152]{1,0:T(8,128)(2,1)S(1)}, u32[]{:S(2)}, u32[]{:S(2)}) collective-permute-start(bf16[216,1152]{1,0:T(8,128)(2,1)S(1)} %constant_dynamic-update-slice_fusion.66), channel_id=1, source_target_pairs={{0,16},{16,0},{1,17},{17,1},{2,18},{18,2},{3,19},{19,3},{4,20},{20... | collective-permute-start | bytes 1493000 | tf_op jit(solution)/shard_map/ppermute | solution.py:17
  70.8 24.2 %collective-permute-start.10 = (bf16[384,1152]{1,0:T(8,128)(2,1)S(1)}, bf16[384,1152]{1,0:T(8,128)(2,1)S(1)}, u32[]{:S(2)}, u32[]{:S(2)}) collective-permute-start(bf16[384,1152]{1,0:T(8,128)(2,1)S(1)} %pad_maximum_fusion.1), channel_id=1, source_target_pairs={{0,16},{16,0},{1,17},{17,1},{2,18},{18,2},{3,19},{19,3},{4,20},{20... | collective-permute-start | bytes 2654216 | tf_op jit(solution)/shard_map/ppermute | solution.py:17
  128.2 6.8 %collective-permute-start.13 = (bf16[144,192]{1,0:T(8,128)(2,1)S(1)}, bf16[144,192]{1,0:T(8,128)(2,1)S(1)}, u32[]{:S(2)}, u32[]{:S(2)}) collective-permute-start(bf16[144,192]{1,0:T(8,128)(2,1)S(1)} %get-tuple-element.225), channel_id=1, source_target_pairs={{0,3},{1,2},{2,1},{3,0},{4,7},{5,6},{6,5},{7,4},{8,11},{9,10},{10,... | collective-permute-start | bytes 165896 | tf_op jit(solution)/shard_map/ppermute | solution.py:13
  129.3 7.0 %collective-permute-start.14 = (bf16[144,192]{1,0:T(8,128)(2,1)S(1)}, bf16[144,192]{1,0:T(8,128)(2,1)S(1)}, u32[]{:S(2)}, u32[]{:S(2)}) collective-permute-start(bf16[144,192]{1,0:T(8,128)(2,1)S(1)} %get-tuple-element.224), channel_id=1, source_target_pairs={{0,4},{1,5},{2,6},{3,7},{4,0},{5,1},{6,2},{7,3},{8,12},{9,13},{10,... | collective-permute-start | bytes 165896 | tf_op jit(solution)/shard_map/ppermute | solution.py:13
  131.8 6.8 %collective-permute-start.16 = (bf16[144,192]{1,0:T(8,128)(2,1)S(1)}, bf16[144,192]{1,0:T(8,128)(2,1)S(1)}, u32[]{:S(2)}, u32[]{:S(2)}) collective-permute-start(bf16[144,192]{1,0:T(8,128)(2,1)S(1)} %get-tuple-element.222), channel_id=1, source_target_pairs={{0,6},{1,7},{2,4},{3,5},{4,2},{5,3},{6,0},{7,1},{8,14},{9,15},{10,... | collective-permute-start | bytes 165896 | tf_op jit(solution)/shard_map/ppermute | solution.py:13
  135.0 6.2 %collective-permute-start.17 = (bf16[144,192]{1,0:T(8,128)(2,1)S(1)}, bf16[144,192]{1,0:T(8,128)(2,1)S(1)}, u32[]{:S(2)}, u32[]{:S(2)}) collective-permute-start(bf16[144,192]{1,0:T(8,128)(2,1)S(1)} %get-tuple-element.221), channel_id=1, source_target_pairs={{0,7},{1,6},{2,5},{3,4},{4,3},{5,2},{6,1},{7,0},{8,15},{9,14},{10,... | collective-permute-start | bytes 165896 | tf_op jit(solution)/shard_map/ppermute | solution.py:13
  143.5 9.8 %collective-permute-start.29 = (bf16[192,1152]{1,0:T(8,128)(2,1)S(1)}, bf16[192,1152]{1,0:T(8,128)(2,1)S(1)}, u32[]{:S(2)}, u32[]{:S(2)}) collective-permute-start(bf16[192,1152]{1,0:T(8,128)(2,1)S(1)} %get-tuple-element.175), channel_id=1, source_target_pairs={{0,1},{1,0},{2,3},{3,2},{4,5},{5,4},{6,7},{7,6},{8,9},{9,8},{10,11... | collective-permute-start | bytes 1327112 | tf_op jit(solution)/shard_map/ppermute | solution.py:13
  144.5 10.7 %collective-permute-start.30 = (bf16[192,1152]{1,0:T(8,128)(2,1)S(1)}, bf16[192,1152]{1,0:T(8,128)(2,1)S(1)}, u32[]{:S(2)}, u32[]{:S(2)}) collective-permute-start(bf16[192,1152]{1,0:T(8,128)(2,1)S(1)} %get-tuple-element.175), channel_id=1, source_target_pairs={{0,2},{1,3},{2,0},{3,1},{4,6},{5,7},{6,4},{7,5},{8,10},{9,11},{10,... | collective-permute-start | bytes 1327112 | tf_op jit(solution)/shard_map/ppermute | solution.py:13
  144.5 24.6 %collective-permute-start.34 = (bf16[576,1152]{1,0:T(8,128)(2,1)}, bf16[576,1152]{1,0:T(8,128)(2,1)}, u32[]{:S(2)}, u32[]{:S(2)}) collective-permute-start(bf16[576,1152]{1,0:T(8,128)(2,1)} %collective-permute-done.33), channel_id=1, source_target_pairs={{0,16},{16,0},{1,17},{17,1},{2,18},{18,2},{3,19},{19,3},{4,20},{20... | collective-permute-start | bytes 3981320 | tf_op jit(solution)/shard_map/ppermute | solution.py:17
  179.7 7.9 %collective-permute-start.35 = (bf16[96,1152]{1,0:T(8,128)(2,1)S(1)}, bf16[96,1152]{1,0:T(8,128)(2,1)S(1)}, u32[]{:S(2)}, u32[]{:S(2)}) collective-permute-start(bf16[96,1152]{1,0:T(8,128)(2,1)S(1)} %get-tuple-element.191), channel_id=1, source_target_pairs={{0,2},{1,3},{2,0},{3,1},{4,6},{5,7},{6,4},{7,5},{8,10},{9,11},{10,... | collective-permute-start | bytes 663560 | tf_op jit(solution)/shard_map/ppermute | solution.py:13
  180.1 7.5 %collective-permute-start.37 = (bf16[96,1152]{1,0:T(8,128)(2,1)S(1)}, bf16[96,1152]{1,0:T(8,128)(2,1)S(1)}, u32[]{:S(2)}, u32[]{:S(2)}) collective-permute-start(bf16[96,1152]{1,0:T(8,128)(2,1)S(1)} %get-tuple-element.190), channel_id=1, source_target_pairs={{0,1},{1,0},{2,3},{3,2},{4,5},{5,4},{6,7},{7,6},{8,9},{9,8},{10,11... | collective-permute-start | bytes 663560 | tf_op jit(solution)/shard_map/ppermute | solution.py:13
  188.9 8.6 %collective-permute-start.38 = (bf16[192,1152]{1,0:T(8,128)(2,1)S(1)}, bf16[192,1152]{1,0:T(8,128)(2,1)S(1)}, u32[]{:S(2)}, u32[]{:S(2)}) collective-permute-start(bf16[192,1152]{1,0:T(8,128)(2,1)S(1)} %pad_maximum_fusion.4), channel_id=1, source_target_pairs={{0,2},{1,3},{2,0},{3,1},{4,6},{5,7},{6,4},{7,5},{8,10},{9,11},{10,... | collective-permute-start | bytes 1327112 | tf_op jit(solution)/shard_map/ppermute | solution.py:13
  191.2 8.4 %collective-permute-start.36 = (bf16[192,1152]{1,0:T(8,128)(2,1)S(1)}, bf16[192,1152]{1,0:T(8,128)(2,1)S(1)}, u32[]{:S(2)}, u32[]{:S(2)}) collective-permute-start(bf16[192,1152]{1,0:T(8,128)(2,1)S(1)} %pad_maximum_fusion.3), channel_id=1, source_target_pairs={{0,1},{1,0},{2,3},{3,2},{4,5},{5,4},{6,7},{7,6},{8,9},{9,8},{10,11... | collective-permute-start | bytes 1327112 | tf_op jit(solution)/shard_map/ppermute | solution.py:13
  (35 other events, 358.8 us)
